TPU v7x, 256 devices: a whole 4x4x8 slice. The times are simulated.
256 devices in a mesh: row: 32 (over x, z_hi, core), col: 8 (over y, z_lo).
Axes of the slice: x: 4, y: 4, z: 8 (z_hi: 4, z_lo: 2; z = z_hi * 2 + z_lo), core: 2. Of those that a mesh axis runs over, the one named last changes fastest.
Arguments:
- image: bfloat16 [1536, 2048, 256], P('row', 'col'), may hold values from -6 to 6
- proj_in: bfloat16 [256, 512], replicated, may hold values from -0.375 to 0.375
- taps_wide: float32 [3, 512], replicated, may hold values from -3 to 3
- taps_tall: float32 [3, 512], replicated, may hold values from -3 to 3
- proj_out: bfloat16 [512, 256], replicated, may hold values from -0.25 to 0.25
- bias: float32 [256], replicated, may hold values from -3 to 3
Outputs:
- result: bfloat16 [1536, 2048, 256], P('row', 'col')
All inputs are finite; a program needn't handle non-finite values.
Results may differ from a plain program's by a relative error of at most 0.0054.
Values may be sent and summed in bfloat16 or wider, within the bound.
A program may use at most 192 MiB of HBM per device.

v0:
```python
import jax
import jax.numpy as jnp
from jax import lax
from jax.sharding import PartitionSpec as P


def extended(cells, sides, width):
    for axis, dim in sides:
        count = lax.axis_size(axis)
        ends = count - 1
        head = lax.slice_in_dim(cells, 0, width, axis=dim)
        tail = lax.slice_in_dim(cells, cells.shape[dim] - width, cells.shape[dim], axis=dim)
        cells = jnp.concatenate(
            [
                lax.ppermute(tail, axis, [(i, (i + 1) % count) for i in range(ends)]),
                cells,
                lax.ppermute(head, axis, [((i + 1) % count, i) for i in range(ends)]),
            ],
            axis=dim,
        )
    return cells


def width_taps(padded, taps):
    return (
        taps[0][:, None] * padded[:, :, :-2]
        + taps[1][:, None] * padded[:, :, 1:-1]
        + taps[2][:, None] * padded[:, :, 2:]
    )


def height_taps(padded, taps):
    return (
        taps[0][:, None] * padded[:-2]
        + taps[1][:, None] * padded[1:-1]
        + taps[2][:, None] * padded[2:]
    )


def on_device(image, proj_in, taps_wide, taps_tall, proj_out, bias):
    lifted = jnp.einsum("hwc,cr->hrw", image, proj_in, preferred_element_type=jnp.float32).astype(
        jnp.bfloat16
    )
    padded = extended(lifted, (("col", 2),), 1)
    widened = width_taps(padded, taps_wide).astype(jnp.bfloat16)
    padded = extended(widened, (("row", 0),), 1)
    heightened = height_taps(padded, taps_tall).astype(jnp.bfloat16)
    mixed = (
        jnp.einsum("hrw,rc->hwc", heightened, proj_out, preferred_element_type=jnp.float32) + bias
    )
    return (image.astype(jnp.float32) + jax.nn.silu(mixed)).astype(jnp.bfloat16)


def solution(mesh):
    in_specs = (P("row", "col", None), P(), P(), P(), P(), P())
    out_specs = P("row", "col", None)
    return jax.shard_map(
        on_device, mesh=mesh, in_specs=in_specs, out_specs=out_specs, check_vma=False
    )
```

profile of v0, /device:TPU:77, one launch (start us, length us, event | category | flops | bytes accessed | tf_op | source)
XLA Modules:
  0.0 85.2 jit_solution(3173379491697955685)
XLA Ops:
  0.0 0.0 copy-start
  0.0 0.0 copy-start.3
  0.0 0.9 %copy-done = bf16[256,512]{1,0:T(8,128)(2,1)S(1)} copy-done((bf16[256,512]{1,0:T(8,128)(2,1)S(1)}, bf16[256,512]{1,0:T(8,128)(2,1)}, u32[]{:S(2)}) %copy-start) | copy-done | bytes 262168
  1.0 9.2 %convert_bitcast_fusion = bf16[48,512,256]{1,2,0:T(8,128)(2,1)} fusion(bf16[48,256,256]{2,1,0:T(8,128)(2,1)} %param.6, bf16[256,512]{1,0:T(8,128)(2,1)S(1)} %copy-done), kind=kOutput, calls=%fused_computation.12 | convolution fusion | flops 3227516928 | bytes 19136512 | tf_op jit(solution)/shard_map/hwc,cr->hrw/dot_general | solution.py:41
  10.1 1.3 %fusion.10 = (bf16[48,512,1]{1,2,0:T(2,128)(2,1)S(1)}, bf16[48,512,1]{1,2,0:T(2,128)(2,1)S(1)}) fusion(bf16[48,512,256]{1,2,0:T(8,128)(2,1)} %convert_bitcast_fusion), kind=kLoop, calls=%fused_computation.18 | loop fusion | bytes 196608 | tf_op jit(solution)/shard_map/slice | solution.py:12
  11.4 3.5 %collective-permute-start = (bf16[48,512,1]{1,2,0:T(2,128)(2,1)S(1)}, bf16[48,512,1]{1,2,0:T(2,128)(2,1)S(1)}, u32[]{:S(2)}, u32[]{:S(2)}) collective-permute-start(bf16[48,512,1]{1,2,0:T(2,128)(2,1)S(1)} %get-tuple-element.7), channel_id=1, source_target_pairs={{0,1},{1,2},{2,3},{3,4},{4,5},{5,6},{6,7},{8,9},{9,10},{10,11},{11... | collective-permute-start | bytes 147464 | tf_op jit(solution)/shard_map/ppermute | solution.py:15
  15.0 2.6 %collective-permute-start.1 = (bf16[48,512,1]{1,2,0:T(2,128)(2,1)S(1)}, bf16[48,512,1]{1,2,0:T(2,128)(2,1)S(1)}, u32[]{:S(2)}, u32[]{:S(2)}) collective-permute-start(bf16[48,512,1]{1,2,0:T(2,128)(2,1)S(1)} %get-tuple-element.8), channel_id=1, source_target_pairs={{1,0},{2,1},{3,2},{4,3},{5,4},{6,5},{7,6},{9,8},{10,9},{11,10},{12... | collective-permute-start | bytes 147464 | tf_op jit(solution)/shard_map/ppermute | solution.py:17
  17.6 0.0 copy-done.3
  17.6 0.0 collective-permute-done
  17.7 2.7 %collective-permute-done.1 = bf16[48,512,1]{1,2,0:T(2,128)(2,1)S(1)} collective-permute-done((bf16[48,512,1]{1,2,0:T(2,128)(2,1)S(1)}, bf16[48,512,1]{1,2,0:T(2,128)(2,1)S(1)}, u32[]{:S(2)}, u32[]{:S(2)}) %collective-permute-start.1) | collective-permute-done | bytes 49184 | tf_op jit(solution)/shard_map/ppermute | solution.py:17
  20.3 0.0 copy-start.4
  20.3 0.0 copy-start.1
  20.3 0.0 copy-start.5
  20.3 0.0 copy-start.6
  20.3 19.1 %add_convert_fusion.1 = bf16[48,512,256]{1,2,0:T(8,128)(2,1)S(1)} fusion(bf16[48,512,256]{1,2,0:T(8,128)(2,1)} %convert_bitcast_fusion, bf16[48,512,1]{1,2,0:T(2,128)(2,1)S(1)} %collective-permute-done.1, bf16[48,512,1]{1,2,0:T(2,128)(2,1)S(1)} %collective-permute-done, f32[512]{0:T(512)S(1)} %bitcast.16, f32[512]{0:T(512)S(1)} %bitcast.17, f32[512]{0:T(512)S(1)} %bitcast.15), kind=kLoop, calls=%fused_computation.1 | loop fusion | flops 94371840 | bytes 25270272 | tf_op jit(solution)/shard_map/convert_element_type | solution.py:45
  39.4 0.0 copy-start.2
  39.4 4.5 %copy-done.2 = bf16[48,512,256]{1,2,0:T(8,128)(2,1)} copy-done((bf16[48,512,256]{1,2,0:T(8,128)(2,1)}, bf16[48,512,256]{1,2,0:T(8,128)(2,1)S(1)}, u32[]{:S(2)}) %copy-start.2) | copy-done | bytes 12582936
  44.0 7.4 %collective-permute-start.2 = (bf16[1,512,256]{1,2,0:T(8,128)(2,1)S(1)}, bf16[1,512,256]{1,2,0:T(8,128)(2,1)S(1)}, u32[]{:S(2)}, u32[]{:S(2)}) collective-permute-start(bf16[1,512,256]{1,2,0:T(8,128)(2,1)S(1)} %get-tuple-element.5), channel_id=1, source_target_pairs={{0,8},{8,16},{16,24},{24,32},{32,40},{40,48},{48,56},{56,64},{64,7... | collective-permute-start | bytes 786440 | tf_op jit(solution)/shard_map/ppermute | solution.py:15
  51.4 1.9 %collective-permute-start.3 = (bf16[1,512,256]{1,2,0:T(8,128)(2,1)S(1)}, bf16[1,512,256]{1,2,0:T(8,128)(2,1)S(1)}, u32[]{:S(2)}, u32[]{:S(2)}) collective-permute-start(bf16[1,512,256]{1,2,0:T(8,128)(2,1)S(1)} %get-tuple-element.6), channel_id=1, source_target_pairs={{8,0},{16,8},{24,16},{32,24},{40,32},{48,40},{56,48},{64,56},{72,6... | collective-permute-start | bytes 786440 | tf_op jit(solution)/shard_map/ppermute | solution.py:17
  53.3 0.0 copy-done.4
  53.3 4.1 %collective-permute-done.2 = bf16[1,512,256]{1,2,0:T(8,128)(2,1)S(1)} collective-permute-done((bf16[1,512,256]{1,2,0:T(8,128)(2,1)S(1)}, bf16[1,512,256]{1,2,0:T(8,128)(2,1)S(1)}, u32[]{:S(2)}, u32[]{:S(2)}) %collective-permute-start.2) | collective-permute-done | bytes 262176 | tf_op jit(solution)/shard_map/ppermute | solution.py:15
  57.4 6.5 %collective-permute-done.3 = bf16[1,512,256]{1,2,0:T(8,128)(2,1)S(1)} collective-permute-done((bf16[1,512,256]{1,2,0:T(8,128)(2,1)S(1)}, bf16[1,512,256]{1,2,0:T(8,128)(2,1)S(1)}, u32[]{:S(2)}, u32[]{:S(2)}) %collective-permute-start.3) | collective-permute-done | bytes 262176 | tf_op jit(solution)/shard_map/ppermute | solution.py:17
  64.0 0.0 copy-done.1
  64.0 0.0 copy-done.5
  64.0 0.0 copy-done.6
  64.0 21.3 %add_convert_fusion.3 = bf16[48,256,256]{2,1,0:T(8,128)(2,1)} fusion(bf16[48,256,256]{2,1,0:T(8,128)(2,1)S(1)} %copy-done.1, f32[256]{0:T(256)S(1)} %copy-done.6, bf16[48,512,256]{1,2,0:T(8,128)(2,1)} %copy-done.2, bf16[1,512,256]{1,2,0:T(8,128)(2,1)S(1)} %collective-permute-done.3, bf16[1,512,256]{1,2,0:T(8,128)(2,1)S(1)} %collective-permute-done.2, ...), kind=kOutput, calls=%fused_computation.9 | convolution fusion | flops 3315597312 | bytes 25959424 | tf_op jit(solution)/shard_map/hrw,rc->hwc/dot_general | solution.py:49
  (3 shorter events, 0.0 us)
Async XLA Ops:
  0.0 1.0 %copy-start = (bf16[256,512]{1,0:T(8,128)(2,1)S(1)}, bf16[256,512]{1,0:T(8,128)(2,1)}, u32[]{:S(2)}) copy-start(bf16[256,512]{1,0:T(8,128)(2,1)} %param.7) | copy-start | bytes 786436
  0.0 17.6 %copy-start.3 = (f32[3,512]{1,0:T(4,128)S(1)}, f32[3,512]{1,0:T(4,128)}, u32[]{:S(2)}) copy-start(f32[3,512]{1,0:T(4,128)} %param.8) | copy-start | bytes 18436
  11.4 6.3 %collective-permute-start = (bf16[48,512,1]{1,2,0:T(2,128)(2,1)S(1)}, bf16[48,512,1]{1,2,0:T(2,128)(2,1)S(1)}, u32[]{:S(2)}, u32[]{:S(2)}) collective-permute-start(bf16[48,512,1]{1,2,0:T(2,128)(2,1)S(1)} %get-tuple-element.7), channel_id=1, source_target_pairs={{0,1},{1,2},{2,3},{3,4},{4,5},{5,6},{6,7},{8,9},{9,10},{10,11},{11... | collective-permute-start | bytes 147464 | tf_op jit(solution)/shard_map/ppermute | solution.py:15
  15.0 5.4 %collective-permute-start.1 = (bf16[48,512,1]{1,2,0:T(2,128)(2,1)S(1)}, bf16[48,512,1]{1,2,0:T(2,128)(2,1)S(1)}, u32[]{:S(2)}, u32[]{:S(2)}) collective-permute-start(bf16[48,512,1]{1,2,0:T(2,128)(2,1)S(1)} %get-tuple-element.8), channel_id=1, source_target_pairs={{1,0},{2,1},{3,2},{4,3},{5,4},{6,5},{7,6},{9,8},{10,9},{11,10},{12... | collective-permute-start | bytes 147464 | tf_op jit(solution)/shard_map/ppermute | solution.py:17
  20.3 33.0 %copy-start.4 = (f32[3,512]{1,0:T(4,128)S(1)}, f32[3,512]{1,0:T(4,128)}, u32[]{:S(2)}) copy-start(f32[3,512]{1,0:T(4,128)} %param.9) | copy-start | bytes 18436
  20.3 43.7 %copy-start.1 = (bf16[48,256,256]{2,1,0:T(8,128)(2,1)S(1)}, bf16[48,256,256]{2,1,0:T(8,128)(2,1)}, u32[]{:S(2)}) copy-start(bf16[48,256,256]{2,1,0:T(8,128)(2,1)} %param.6) | copy-start | bytes 18874372
  20.3 43.7 %copy-start.5 = (bf16[512,256]{1,0:T(8,128)(2,1)S(1)}, bf16[512,256]{1,0:T(8,128)(2,1)}, u32[]{:S(2)}) copy-start(bf16[512,256]{1,0:T(8,128)(2,1)} %param.10) | copy-start | bytes 786436
  20.3 43.7 %copy-start.6 = (f32[256]{0:T(256)S(1)}, f32[256]{0:T(256)}, u32[]{:S(2)}) copy-start(f32[256]{0:T(256)} %param.11) | copy-start | bytes 3076
  39.4 4.5 %copy-start.2 = (bf16[48,512,256]{1,2,0:T(8,128)(2,1)}, bf16[48,512,256]{1,2,0:T(8,128)(2,1)S(1)}, u32[]{:S(2)}) copy-start(bf16[48,512,256]{1,2,0:T(8,128)(2,1)S(1)} %add_convert_fusion.1) | copy-start | bytes 37748740
  44.0 13.5 %collective-permute-start.2 = (bf16[1,512,256]{1,2,0:T(8,128)(2,1)S(1)}, bf16[1,512,256]{1,2,0:T(8,128)(2,1)S(1)}, u32[]{:S(2)}, u32[]{:S(2)}) collective-permute-start(bf16[1,512,256]{1,2,0:T(8,128)(2,1)S(1)} %get-tuple-element.5), channel_id=1, source_target_pairs={{0,8},{8,16},{16,24},{24,32},{32,40},{40,48},{48,56},{56,64},{64,7... | collective-permute-start | bytes 786440 | tf_op jit(solution)/shard_map/ppermute | solution.py:15
  51.4 12.6 %collective-permute-start.3 = (bf16[1,512,256]{1,2,0:T(8,128)(2,1)S(1)}, bf16[1,512,256]{1,2,0:T(8,128)(2,1)S(1)}, u32[]{:S(2)}, u32[]{:S(2)}) collective-permute-start(bf16[1,512,256]{1,2,0:T(8,128)(2,1)S(1)} %get-tuple-element.6), channel_id=1, source_target_pairs={{8,0},{16,8},{24,16},{32,24},{40,32},{48,40},{56,48},{64,56},{72,6... | collective-permute-start | bytes 786440 | tf_op jit(solution)/shard_map/ppermute | solution.py:17
where the time goes:
time: 85.5 us; the launch traced here: 85.2 us
  matrix products  30.4 us (36%)
  other arithmetic  19.1 us (22%)
  starting transfers between devices  15.5 us (18%)
  waiting for transfers between devices  13.3 us (16%)
  local copies, waits for them, and re-layouts  6.81 us (8%)
    dot_general x1, matrix products, on_device(): jnp.einsum('hrw,rc->hwc', heightened, proj_out, preferred_element_type=jn...  21.3 us
    convert_element_type x1, other arithmetic, on_device(): widened = width_taps(padded, taps_wide).astype(jnp.bfloat16)  19.1 us
    ppermute x2, starting transfers between devices, extended(): lax.ppermute(tail, axis, [(i, (i + 1) % count) for i in range(ends)])  10.9 us
    ppermute x2, waiting for transfers between devices, extended(): lax.ppermute(head, axis, [((i + 1) % count, i) for i in range(ends)])  9.2 us
    dot_general x1, matrix products, on_device(): jnp.einsum('hwc,cr->hrw', image, proj_in, preferred_element_type=jnp.floa...  9.18 us
    unnamed x14, local copies, waits for them, and re-layouts  5.49 us
    ppermute x2, starting transfers between devices, extended(): lax.ppermute(head, axis, [((i + 1) % count, i) for i in range(ends)])  4.56 us
    ppermute x2, waiting for transfers between devices, extended(): lax.ppermute(tail, axis, [(i, (i + 1) % count) for i in range(ends)])  4.15 us
  transfers between devices with their start and end apart: 4, of which 3 were waited for; matrix products, arithmetic and copies ran while one was open for 0% of the time, Pallas kernels for 0%

commit v1 on v0

v1 whole, which is shorter than its diff:
```python
import functools

import jax
import jax.numpy as jnp
from jax import lax
from jax.experimental import pallas as pl
from jax.experimental.pallas import tpu as pltpu
from jax.sharding import PartitionSpec as P

MESH = pl.DeviceIdType.MESH
F32, BF16 = jnp.float32, jnp.bfloat16
EDGE = 16
STAGES = 3
PAIRS = 3


def spread_kernel(
    rows, cols,
    image, proj_in, taps_wide, taps_tall, proj_out,
    centre, left, right, weights,
    strip_l, strip_r, edge_l, edge_r, halo_l, halo_r, corners, halo_lf, halo_rf, p_in, t_wide, t_tall, p_out,
    local_sem, stage_sem, send_sem, recv_sem,
):
    th, tw, c = image.shape
    r, k = lax.axis_index("row"), lax.axis_index("col")
    up, down = lax.rem(r + rows - 1, rows), lax.rem(r + 1, rows)
    west, east = lax.rem(k + cols - 1, cols), lax.rem(k + 1, cols)
    around = [(up, k), (down, k), (r, west), (r, east), (up, west), (up, east), (down, west), (down, east)]

    barrier = pltpu.get_barrier_semaphore()
    for to in around:
        pl.semaphore_signal(barrier, inc=1, device_id=to, device_id_type=MESH)

    local = [
        pltpu.make_async_copy(src, dst, local_sem.at[i])
        for i, (src, dst) in enumerate([
            (image.at[:, pl.ds(0, EDGE)], strip_l),
            (image.at[:, pl.ds(tw - EDGE, EDGE)], strip_r),
            (proj_in, p_in), (taps_wide, t_wide), (taps_tall, t_tall), (proj_out, p_out),
        ])
    ]
    for copy in local:
        copy.start()
    step = th // STAGES

    def stage(s):
        return pltpu.make_async_copy(image.at[pl.ds(s * step, step)], centre.at[pl.ds(1 + s * step, step)], stage_sem.at[s])

    for s in range(STAGES):
        stage(s).start()

    pl.semaphore_wait(barrier, len(around))

    def send(i, src, dst, to):
        copy = pltpu.make_async_remote_copy(
            src_ref=src, dst_ref=dst, send_sem=send_sem.at[i], recv_sem=recv_sem.at[i], device_id=to, device_id_type=MESH
        )
        copy.start()
        return copy

    row_copies = [
        send(0, image.at[0], centre.at[th + 1], (up, k)),
        send(1, image.at[th - 1], centre.at[0], (down, k)),
    ]
    local[0].wait()
    local[1].wait()
    edge_l[...] = strip_l[:, 0, :]
    edge_r[...] = strip_r[:, EDGE - 1, :]
    top, bottom = pl.ds(0, EDGE), pl.ds(th - EDGE, EDGE)
    edge_copies = [
        send(2, edge_l, halo_r, (r, west)),
        send(3, edge_r, halo_l, (r, east)),
        send(4, edge_l.at[top], corners.at[0], (up, west)),
        send(5, edge_r.at[top], corners.at[1], (up, east)),
        send(6, edge_l.at[bottom], corners.at[2], (down, west)),
        send(7, edge_r.at[bottom], corners.at[3], (down, east)),
    ]
    for copy in local[2:]:
        copy.wait()

    def shift(h, before, after):
        v = centre[h]
        p = jnp.concatenate([v[1:], after], 0)
        right[h] = p
        left[h] = jnp.concatenate([before, v[:1], p[:-2]], 0)

    zero = jnp.zeros((1, c), BF16)

    def taps(j, carry):
        stage(j).wait()
        wide = t_wide[pl.ds(j, 1)]
        base = p_in[...].astype(F32)
        g = []
        for i in range(3):
            a = base * (wide * t_tall[pl.ds(i, 1)])
            high = a.astype(BF16)
            low = (a - high.astype(F32)).astype(BF16)
            g.append(
                jnp.dot(high, p_out[...], preferred_element_type=F32) + jnp.dot(low, p_out[...], preferred_element_type=F32)
            )
        at = pl.ds(pl.multiple_of(j * c, c), c)
        ends = 0.25 * (g[0] + g[2])
        middle = 0.25 * g[1]
        weights[0, at] = (0.5 * g[0]).astype(BF16)
        weights[1, at] = (ends + middle).astype(BF16)
        weights[2, at] = (ends - middle).astype(BF16)
        weights[3, at] = (0.5 * g[2]).astype(BF16)
        for h in range(step):
            shift(1 + j * step + h, zero, zero)
        return carry

    lax.fori_loop(0, STAGES, taps, 0)

    for copy in edge_copies:
        copy.wait()
    halo_lf[...] = jnp.where(k > 0, halo_l[...].astype(F32), 0.0)
    halo_rf[...] = jnp.where(k < cols - 1, halo_r[...].astype(F32), 0.0)
    line = lax.broadcasted_iota(jnp.int32, (EDGE, c), 0)

    def mend(h, carry):
        tile = left[h + 1, pl.ds(0, EDGE)].astype(F32)
        left[h + 1, pl.ds(0, EDGE)] = jnp.where(line == 0, halo_lf[pl.ds(h, 1)], tile).astype(BF16)
        tile = right[h + 1, pl.ds(tw - EDGE, EDGE)].astype(F32)
        right[h + 1, pl.ds(tw - EDGE, EDGE)] = jnp.where(line == EDGE - 1, halo_rf[pl.ds(h, 1)], tile).astype(BF16)
        return carry

    lax.fori_loop(0, th, mend, 0)

    for copy in row_copies:
        copy.wait()

    def corner(i, at, edge):
        return jnp.where(edge, 0.0, corners[i].astype(F32))[at : at + 1].astype(BF16)

    @pl.when(r == 0)
    def _():
        centre[0] = jnp.zeros((tw, c), BF16)

    @pl.when(r == rows - 1)
    def _():
        centre[th + 1] = jnp.zeros((tw, c), BF16)

    shift(0, corner(3, EDGE - 1, (k == 0) | (r == 0)), corner(2, EDGE - 1, (k == cols - 1) | (r == 0)))
    shift(th + 1, corner(1, 0, (k == 0) | (r == rows - 1)), corner(0, 0, (k == cols - 1) | (r == rows - 1)))


def spread(rows, cols, image, proj_in, taps_wide, taps_tall, proj_out):
    th, tw, c = image.shape
    rank = proj_in.shape[1]
    vmem, hbm = pl.BlockSpec(memory_space=pltpu.VMEM), pl.BlockSpec(memory_space=pltpu.HBM)
    tile = jax.ShapeDtypeStruct((th + 2, tw, c), BF16)
    return pl.pallas_call(
        functools.partial(spread_kernel, rows, cols),
        out_shape=(tile, tile, tile, jax.ShapeDtypeStruct((4, 3 * c, c), BF16)),
        in_specs=[hbm] * 5,
        out_specs=(vmem,) * 4,
        scratch_shapes=[
            pltpu.VMEM((th, EDGE, c), BF16),
            pltpu.VMEM((th, EDGE, c), BF16),
            pltpu.VMEM((th, c), BF16),
            pltpu.VMEM((th, c), BF16),
            pltpu.VMEM((th, c), BF16),
            pltpu.VMEM((th, c), BF16),
            pltpu.VMEM((4, EDGE, c), BF16),
            pltpu.VMEM((th, c), F32),
            pltpu.VMEM((th, c), F32),
            pltpu.VMEM((c, rank), BF16),
            pltpu.VMEM((3, rank), F32),
            pltpu.VMEM((3, rank), F32),
            pltpu.VMEM((rank, c), BF16),
            pltpu.SemaphoreType.DMA((6,)),
            pltpu.SemaphoreType.DMA((STAGES,)),
            pltpu.SemaphoreType.DMA((8,)),
            pltpu.SemaphoreType.DMA((8,)),
        ],
        compiler_params=pltpu.CompilerParams(collective_id=0, has_side_effects=True, vmem_limit_bytes=32 * 2**20),
        cost_estimate=pl.CostEstimate(flops=18 * 2 * c * c * rank, bytes_accessed=8 * th * tw * c, transcendentals=0),
        name="spread",
    )(image, proj_in, taps_wide, taps_tall, proj_out)


def convolve_kernel(centre, left, right, weights, bias, out):
    chunk, tw, c = out.shape
    first = pl.program_id(0) * chunk
    half = 0.5 * bias[...]

    def moved(k):
        columns = []
        for ref in (left, centre, right):
            parts = []
            for q in range(PAIRS):
                d = [ref.at[first + 2 * q + i] for i in range(4)]
                if k == 0:
                    parts.append(d[0][...] - d[2][...])
                elif k == 1:
                    parts.append(d[1][...] + d[2][...])
                elif k == 2:
                    parts.append(d[2][...] - d[1][...])
                else:
                    parts.append(d[1][...] - d[3][...])
            columns.append(jnp.concatenate(parts, 0))
        return jnp.concatenate(columns, 1)

    def product(k):
        return jnp.dot(moved(k), weights[k], preferred_element_type=F32)

    def finish(y, i):
        t = y + half
        s = t + t * jnp.tanh(t)
        for q in range(PAIRS):
            o = centre[first + 2 * q + i + 1].astype(F32) + s[q * tw : (q + 1) * tw]
            out[2 * q + i] = o.astype(BF16)

    m1, m2 = product(1), product(2)
    total, difference = m1 + m2, m1 - m2
    finish(total + product(0), 0)
    finish(difference - product(3), 1)


def convolve(centre, left, right, weights, bias):
    th, tw, c = centre.shape
    th -= 2
    chunk = 2 * PAIRS
    vmem = pl.BlockSpec(memory_space=pltpu.VMEM)
    return pl.pallas_call(
        convolve_kernel,
        grid=(th // chunk,),
        out_shape=jax.ShapeDtypeStruct((th, tw, c), BF16),
        in_specs=[vmem] * 5,
        out_specs=pl.BlockSpec((chunk, tw, c), lambda i: (i, 0, 0)),
        compiler_params=pltpu.CompilerParams(vmem_limit_bytes=32 * 2**20),
        cost_estimate=pl.CostEstimate(flops=2 * 6 * th * tw * c * c, bytes_accessed=2 * th * tw * c, transcendentals=th * tw * c),
        name="convolve",
    )(centre, left, right, weights, bias)


def solution(mesh):
    rows, cols = mesh.shape["row"], mesh.shape["col"]

    def on_device(image, proj_in, taps_wide, taps_tall, proj_out, bias):
        tiles = spread(rows, cols, image, proj_in, taps_wide, taps_tall, proj_out)
        return convolve(*tiles, bias[None, :])

    in_specs = (P("row", "col", None), P(), P(), P(), P(), P())
    out_specs = P("row", "col", None)
    return jax.shard_map(on_device, mesh=mesh, in_specs=in_specs, out_specs=out_specs, check_vma=False)
```

time: 85.5 us -> 48.8 us (0.57)
  the two profiles are of different devices: /device:TPU:77 before, /device:TPU:1 now
where the time goes in v1:
time: 48.8 us; the launch traced here: 48.5 us
  Pallas kernels  34 us (70%)
  local copies, waits for them, and re-layouts  14.5 us (30%)
    pallas_call x1, Pallas kernels, spread(): pl.pallas_call(functools.partial(spread_kernel, rows, cols), out_shape=(t...  20 us
    unnamed x18, local copies, waits for them, and re-layouts  14.5 us
    pallas_call x1, Pallas kernels, convolve(): pl.pallas_call(convolve_kernel, grid=(th // chunk,), out_shape=jax.ShapeD...  14 us

profile of v1, /device:TPU:1, one launch (start us, length us, event | category | flops | bytes accessed | tf_op | source)
XLA Modules:
  0.0 48.5 jit_solution(3539012714368086796)
XLA Ops:
  0.0 0.0 copy-start.8
  0.0 0.0 copy-start
  0.0 2.8 %copy-done = bf16[48,256,256]{2,1,0:T(8,128)(2,1)S(1)} copy-done((bf16[48,256,256]{2,1,0:T(8,128)(2,1)S(1)}, bf16[48,256,256]{2,1,0:T(8,128)(2,1)}, u32[]{:S(2)}) %copy-start) | copy-done | bytes 6291480
  2.8 0.0 copy-start.1
  2.8 0.9 %copy-done.1 = bf16[256,512]{1,0:T(8,128)(2,1)S(1)} copy-done((bf16[256,512]{1,0:T(8,128)(2,1)S(1)}, bf16[256,512]{1,0:T(8,128)(2,1)}, u32[]{:S(2)}) %copy-start.1) | copy-done | bytes 262168
  3.8 0.0 copy-start.2
  3.8 0.9 %copy-done.2 = bf16[512,256]{1,0:T(8,128)(2,1)S(1)} copy-done((bf16[512,256]{1,0:T(8,128)(2,1)S(1)}, bf16[512,256]{1,0:T(8,128)(2,1)}, u32[]{:S(2)}) %copy-start.2) | copy-done | bytes 262168
  4.7 0.0 copy-start.3
  4.7 0.7 %copy-done.3 = f32[3,512]{1,0:T(4,128)S(1)} copy-done((f32[3,512]{1,0:T(4,128)S(1)}, f32[3,512]{1,0:T(4,128)}, u32[]{:S(2)}) %copy-start.3) | copy-done | bytes 6168
  5.4 0.0 copy-start.4
  5.4 0.7 %copy-done.4 = f32[3,512]{1,0:T(4,128)S(1)} copy-done((f32[3,512]{1,0:T(4,128)S(1)}, f32[3,512]{1,0:T(4,128)}, u32[]{:S(2)}) %copy-start.4) | copy-done | bytes 6168
  6.1 20.0 %spread.1 = (bf16[50,256,256]{2,1,0:T(8,128)(2,1)S(1)}, bf16[50,256,256]{2,1,0:T(8,128)(2,1)S(1)}, bf16[50,256,256]{2,1,0:T(8,128)(2,1)}, bf16[4,768,256]{2,1,0:T(8,128)(2,1)S(1)}) custom-call(bf16[48,256,256]{2,1,0:T(8,128)(2,1)S(1)} %copy-done, bf16[256,512]{1,0:T(8,128)(2,1)S(1)} %copy-done.1, f32[3,512]{1,0:T(4,128)S(1)} %copy-done.3, ...), custom_call_target="tpu_custom_call" | custom-call | flops 1207959552 | bytes 25165824 | tf_op jit(solution)/shard_map/spread/pallas_call | solution.py:152
  26.1 0.0 copy-start.5
  26.1 2.7 %copy-done.5 = bf16[50,256,256]{2,1,0:T(8,128)(2,1)} copy-done((bf16[50,256,256]{2,1,0:T(8,128)(2,1)}, bf16[50,256,256]{2,1,0:T(8,128)(2,1)S(1)}, u32[]{:S(2)}) %copy-start.5) | copy-done | bytes 6553624
  28.8 0.0 copy-done.8
  28.8 0.0 copy-start.6
  28.8 2.9 %copy-done.6 = bf16[50,256,256]{2,1,0:T(8,128)(2,1)S(1)} copy-done((bf16[50,256,256]{2,1,0:T(8,128)(2,1)S(1)}, bf16[50,256,256]{2,1,0:T(8,128)(2,1)}, u32[]{:S(2)}) %copy-start.6) | copy-done | bytes 6553624
  31.7 0.0 copy-start.7
  31.7 2.9 %copy-done.7 = bf16[50,256,256]{2,1,0:T(8,128)(2,1)S(1)} copy-done((bf16[50,256,256]{2,1,0:T(8,128)(2,1)S(1)}, bf16[50,256,256]{2,1,0:T(8,128)(2,1)}, u32[]{:S(2)}) %copy-start.7) | copy-done | bytes 6553624
  34.5 14.0 %convolve.1 = bf16[48,256,256]{2,1,0:T(8,128)(2,1)} custom-call(bf16[50,256,256]{2,1,0:T(8,128)(2,1)S(1)} %get-tuple-element.9.centre, bf16[50,256,256]{2,1,0:T(8,128)(2,1)S(1)} %copy-done.6, bf16[50,256,256]{2,1,0:T(8,128)(2,1)S(1)} %copy-done.7, bf16[4,768,256]{2,1,0:T(8,128)(2,1)S(1)} %get-tuple-element.12.weights, f32[1,256]{1,0:T(1,128)S(1)} %bitcast.1), custom_call_target="tpu_custom_call" | custom-call | flops 9663676416 | bytes 6291456 | tf_op jit(solution)/shard_map/convolve/pallas_call | solution.py:225
Async XLA Ops:
  0.0 28.8 %copy-start.8 = (f32[256]{0:T(256)S(1)}, f32[256]{0:T(256)}, u32[]{:S(2)}) copy-start(f32[256]{0:T(256)} %param.11) | copy-start | bytes 3076
  0.0 2.8 %copy-start = (bf16[48,256,256]{2,1,0:T(8,128)(2,1)S(1)}, bf16[48,256,256]{2,1,0:T(8,128)(2,1)}, u32[]{:S(2)}) copy-start(bf16[48,256,256]{2,1,0:T(8,128)(2,1)} %image.1) | copy-start | bytes 18874372
  2.8 0.9 %copy-start.1 = (bf16[256,512]{1,0:T(8,128)(2,1)S(1)}, bf16[256,512]{1,0:T(8,128)(2,1)}, u32[]{:S(2)}) copy-start(bf16[256,512]{1,0:T(8,128)(2,1)} %proj_in.1) | copy-start | bytes 786436
  3.8 0.9 %copy-start.2 = (bf16[512,256]{1,0:T(8,128)(2,1)S(1)}, bf16[512,256]{1,0:T(8,128)(2,1)}, u32[]{:S(2)}) copy-start(bf16[512,256]{1,0:T(8,128)(2,1)} %proj_out.1) | copy-start | bytes 786436
  4.7 0.7 %copy-start.3 = (f32[3,512]{1,0:T(4,128)S(1)}, f32[3,512]{1,0:T(4,128)}, u32[]{:S(2)}) copy-start(f32[3,512]{1,0:T(4,128)} %taps_wide.1) | copy-start | bytes 18436
  5.4 0.7 %copy-start.4 = (f32[3,512]{1,0:T(4,128)S(1)}, f32[3,512]{1,0:T(4,128)}, u32[]{:S(2)}) copy-start(f32[3,512]{1,0:T(4,128)} %taps_tall.1) | copy-start | bytes 18436
  26.1 2.7 %copy-start.5 = (bf16[50,256,256]{2,1,0:T(8,128)(2,1)}, bf16[50,256,256]{2,1,0:T(8,128)(2,1)S(1)}, u32[]{:S(2)}) copy-start(bf16[50,256,256]{2,1,0:T(8,128)(2,1)S(1)} %get-tuple-element.10.left) | copy-start | bytes 19660804
  28.8 2.9 %copy-start.6 = (bf16[50,256,256]{2,1,0:T(8,128)(2,1)S(1)}, bf16[50,256,256]{2,1,0:T(8,128)(2,1)}, u32[]{:S(2)}) copy-start(bf16[50,256,256]{2,1,0:T(8,128)(2,1)} %copy-done.5) | copy-start | bytes 19660804
  31.7 2.9 %copy-start.7 = (bf16[50,256,256]{2,1,0:T(8,128)(2,1)S(1)}, bf16[50,256,256]{2,1,0:T(8,128)(2,1)}, u32[]{:S(2)}) copy-start(bf16[50,256,256]{2,1,0:T(8,128)(2,1)} %get-tuple-element.11.right) | copy-start | bytes 19660804

commit v2 on v0

v2 whole, which is shorter than its diff:
```python
import functools

import jax
import jax.numpy as jnp
from jax import lax
from jax.experimental import pallas as pl
from jax.experimental.pallas import tpu as pltpu
from jax.sharding import PartitionSpec as P

MESH = pl.DeviceIdType.MESH
F32, BF16 = jnp.float32, jnp.bfloat16
EDGE = 16
PAIRS = 3
SPAN = 2 * PAIRS
DEEP = SPAN + 2


def products(pick, weights):
    def moved(k):
        columns = []
        for side in range(3):
            parts = []
            for q in range(PAIRS):
                a, b = ((0, 2), (1, 2), (2, 1), (1, 3))[k]
                a, b = pick(side, q, a), pick(side, q, b)
                parts.append(a + b if k == 1 else a - b)
            columns.append(jnp.concatenate(parts, 0))
        return jnp.concatenate(columns, 1)

    def product(k):
        return jnp.dot(moved(k), weights[k], preferred_element_type=F32)

    m1, m2 = product(1), product(2)
    total, difference = m1 + m2, m1 - m2
    return total + product(0), difference - product(3)


def activated(t):
    return t + t * jnp.tanh(t)


def get_rows(ref, at):
    return jnp.concatenate([ref[n, at] for n in range(ref.shape[0])], 1)


def put_rows(ref, at, value):
    wide = ref.shape[2]
    for n in range(ref.shape[0]):
        ref[n, at] = value[:, n * wide : (n + 1) * wide]


def shifted(v, before, after):
    p = jnp.concatenate([v[1:], after], 0)
    return jnp.concatenate([before, v[:1], p[:-2]], 0), p


def interior_kernel(
    rows, cols,
    image, proj_in, taps_wide, taps_tall, proj_out, bias,
    centre, done, last_l, last_r, weights,
    left_a, left_b, right_a, right_b, sum_a, sum_b,
    strip_l, strip_r, edge_l, edge_r, halo_l, halo_r, corners, column_l, column_r, before_l, before_r, fixed_l, fixed_r, own_l, own_r,
    p_in, t_wide, t_tall, p_out,
    local_sem, stage_sem, send_sem, recv_sem,
):
    th, tw, c = image.shape
    steps = th // SPAN - 1
    r, k = lax.axis_index("row"), lax.axis_index("col")
    up, down = lax.rem(r + rows - 1, rows), lax.rem(r + 1, rows)
    west, east = lax.rem(k + cols - 1, cols), lax.rem(k + 1, cols)
    around = [(up, k), (down, k), (r, west), (r, east), (up, west), (up, east), (down, west), (down, east)]

    barrier = pltpu.get_barrier_semaphore()
    for to in around:
        pl.semaphore_signal(barrier, inc=1, device_id=to, device_id_type=MESH)

    def stage(s):
        return pltpu.make_async_copy(image.at[pl.ds(s * SPAN, SPAN)], centre.at[pl.ds(1 + s * SPAN, SPAN)], stage_sem.at[s])

    stages = th // SPAN
    local = [
        pltpu.make_async_copy(src, dst, local_sem.at[i])
        for i, (src, dst) in enumerate([
            (proj_in, p_in), (taps_wide, t_wide), (taps_tall, t_tall), (proj_out, p_out),
            (image.at[:, pl.ds(0, EDGE)], strip_l),
            (image.at[:, pl.ds(tw - EDGE, EDGE)], strip_r),
        ])
    ]
    for copy in local[:4]:
        copy.start()
    for s in range(2):
        stage(s).start()
    for copy in local[4:]:
        copy.start()
    for s in range(2, stages):
        stage(s).start()

    zero = jnp.zeros((1, c), BF16)
    half = 0.5 * bias[...]

    def shift(at, left, right, i):
        left[i], right[i] = shifted(centre[at], zero, zero)

    for copy in local[:4]:
        copy.wait()
    for s in range(2):
        stage(s).wait()

    base = p_in[...].astype(F32)
    for j in range(3):
        wide = t_wide[pl.ds(j, 1)]
        g = []
        for i in range(3):
            a = base * (wide * t_tall[pl.ds(i, 1)])
            high = a.astype(BF16)
            low = (a - high.astype(F32)).astype(BF16)
            g.append(
                jnp.dot(high, p_out[...], preferred_element_type=F32) + jnp.dot(low, p_out[...], preferred_element_type=F32)
            )
        at = pl.ds(j * c, c)
        ends = 0.25 * (g[0] + g[2])
        middle = 0.25 * g[1]
        weights[0, at] = (0.5 * g[0]).astype(BF16)
        weights[1, at] = (ends + middle).astype(BF16)
        weights[2, at] = (ends - middle).astype(BF16)
        weights[3, at] = (0.5 * g[2]).astype(BF16)
        for i in range(j * DEEP // 3, (j + 1) * DEEP // 3):
            shift(2 + i, left_a, right_a, i)

    def multiply(s, left, right, total):
        first = 2 + SPAN * s

        def pick(side, q, i):
            if side == 1:
                return centre[first + 2 * q + i]
            return (left, None, right)[side][2 * q + i]

        total[0], total[1] = products(pick, weights)

    def finish(s, total):
        first = 2 + SPAN * s
        for i in range(2):
            t = total[i] + half
            y = activated(t)
            for q in range(PAIRS):
                row = first + 2 * q + i
                pair = pl.ds(1 + PAIRS * s + q, 1)
                done[row] = (centre[row + 1].astype(F32) + y[q * tw : (q + 1) * tw]).astype(BF16)
                before_l[i, pair] = t[q * tw : q * tw + 1]
                before_r[i, pair] = t[(q + 1) * tw - 1 : (q + 1) * tw]

    def prepare(s, left, right, old_left, old_right):
        for i in range(2):
            left[i] = old_left[SPAN + i]
            right[i] = old_right[SPAN + i]
        for i in range(2, DEEP):
            shift(jnp.minimum(2 + SPAN * s + i, th), left, right, i)

    stage(2).wait()
    multiply(0, left_a, right_a, sum_a)
    prepare(1, left_b, right_b, left_a, right_a)

    for copy in local[4:]:
        copy.wait()
    edge_l[...] = strip_l[:, 0, :]
    edge_r[...] = strip_r[:, EDGE - 1, :]
    for s in range(3, stages):
        stage(s).wait()

    pl.semaphore_wait(barrier, len(around))

    def send(i, src, dst, to):
        copy = pltpu.make_async_remote_copy(
            src_ref=src, dst_ref=dst, send_sem=send_sem.at[i], recv_sem=recv_sem.at[i], device_id=to, device_id_type=MESH
        )
        copy.start()
        return copy

    top, bottom = pl.ds(0, EDGE), pl.ds(th - EDGE, EDGE)
    row_copies = [
        send(0, image.at[0], centre.at[th + 1], (up, k)),
        send(1, image.at[th - 1], centre.at[0], (down, k)),
    ]
    edge_copies = [
        send(2, edge_l, halo_r, (r, west)),
        send(3, edge_r, halo_l, (r, east)),
        send(4, edge_l.at[top], corners.at[0], (up, west)),
        send(5, edge_r.at[top], corners.at[1], (up, east)),
        send(6, edge_l.at[bottom], corners.at[2], (down, west)),
        send(7, edge_r.at[bottom], corners.at[3], (down, east)),
    ]

    def two(n, carry):
        s = 2 * n + 1
        multiply(s, left_b, right_b, sum_b)
        finish(s - 1, sum_a)
        prepare(s + 1, left_a, right_a, left_b, right_b)
        multiply(s + 1, left_a, right_a, sum_a)
        finish(s, sum_b)
        prepare(s + 2, left_b, right_b, left_a, right_a)
        return carry

    lax.fori_loop(0, (steps - 1) // 2, two, 0)
    finish(steps - 1, sum_a)

    held = [*range(4), *range(th - SPAN + 2, th + 2)]
    for i, at in enumerate(held):
        if 0 < at <= th:
            shift(at, last_l, last_r, i)

    for copy in edge_copies:
        copy.wait()

    pairs = before_l.shape[1]
    fixed = []
    for side, (halo, column, edge, own, before, new, at, low, high) in enumerate([
        (halo_l, column_l, edge_l, own_l, before_l, fixed_l, 0, 3, 1),
        (halo_r, column_r, edge_r, own_r, before_r, fixed_r, 2 * c, 2, 0),
    ]):
        out_of_image = (k == 0) if side == 0 else (k == cols - 1)
        column[...] = jnp.zeros_like(column)
        put_rows(column, pl.ds(8, th), jnp.where(out_of_image, 0.0, halo[...].astype(F32)))
        upper = jnp.where(out_of_image | (r == 0), 0.0, corners[low].astype(F32))
        lower = jnp.where(out_of_image | (r == rows - 1), 0.0, corners[high].astype(F32))
        put_rows(column, pl.ds(7, 1), upper[EDGE - 1 :])
        put_rows(column, pl.ds(8 + th, 1), lower[:1])
        own[...] = jnp.zeros_like(own)
        put_rows(own, pl.ds(0, th), edge[...].astype(F32))
        d = [get_rows(column, pl.ds(7 + i, pairs, stride=2)) for i in range(4)]
        m = [
            jnp.dot(v.astype(BF16), weights[i, pl.ds(at, c)], preferred_element_type=F32)
            for i, v in enumerate([d[0] - d[2], d[1] + d[2], d[2] - d[1], d[1] - d[3]])
        ]
        for i, y in enumerate([m[0] + m[1] + m[2], m[1] - m[2] - m[3]]):
            lines = pl.ds(i, pairs, stride=2)
            put_rows(new, lines, get_rows(own, lines) + activated(before[i] + y))

    line = lax.broadcasted_iota(jnp.int32, (EDGE, c), 0)

    def placed(ref, h, start, where, value):
        tile = ref[h, pl.ds(start, EDGE)].astype(F32)
        ref[h, pl.ds(start, EDGE)] = jnp.where(line == where, value, tile).astype(BF16)

    def mend(h, carry):
        placed(done, h, 0, 0, get_rows(fixed_l, pl.ds(h, 1)))
        placed(done, h, tw - EDGE, EDGE - 1, get_rows(fixed_r, pl.ds(h, 1)))
        return carry

    lax.fori_loop(2, 2 + SPAN * steps, mend, 0)

    for copy in row_copies:
        copy.wait()

    @pl.when(r == 0)
    def _():
        centre[0] = jnp.zeros((tw, c), BF16)

    @pl.when(r == rows - 1)
    def _():
        centre[th + 1] = jnp.zeros((tw, c), BF16)

    for i, at in enumerate(held):
        if not 0 < at <= th:
            shift(at, last_l, last_r, i)
    for i, at in enumerate(held):
        placed(last_l, i, 0, 0, get_rows(column_l, pl.ds(7 + at, 1)))
        placed(last_r, i, tw - EDGE, EDGE - 1, get_rows(column_r, pl.ds(7 + at, 1)))


def interior(rows, cols, image, proj_in, taps_wide, taps_tall, proj_out, bias):
    th, tw, c = image.shape
    rank = proj_in.shape[1]
    pairs = -(-th // 32) * 16
    vmem, hbm = pl.BlockSpec(memory_space=pltpu.VMEM), pl.BlockSpec(memory_space=pltpu.HBM)
    return pl.pallas_call(
        functools.partial(interior_kernel, rows, cols),
        out_shape=(
            jax.ShapeDtypeStruct((th + 2, tw, c), BF16),
            jax.ShapeDtypeStruct((th, tw, c), BF16),
            jax.ShapeDtypeStruct((SPAN + 4, tw, c), BF16),
            jax.ShapeDtypeStruct((SPAN + 4, tw, c), BF16),
            jax.ShapeDtypeStruct((4, 3 * c, c), BF16),
        ),
        in_specs=[hbm] * 5 + [vmem],
        out_specs=(vmem,) * 5,
        scratch_shapes=[pltpu.VMEM((DEEP, tw, c), BF16)] * 4
        + [pltpu.VMEM((2, PAIRS * tw, c), F32)] * 2
        + [pltpu.VMEM((th, EDGE, c), BF16)] * 2
        + [pltpu.VMEM((th, c), BF16)] * 4
        + [pltpu.VMEM((4, EDGE, c), BF16)]
        + [pltpu.VMEM((c // 128, 2 * pairs + 16, 128), F32)] * 2
        + [pltpu.VMEM((2, pairs, c), F32)] * 2
        + [pltpu.VMEM((c // 128, 2 * pairs, 128), F32)] * 4
        + [
            pltpu.VMEM((c, rank), BF16),
            pltpu.VMEM((3, rank), F32),
            pltpu.VMEM((3, rank), F32),
            pltpu.VMEM((rank, c), BF16),
            pltpu.SemaphoreType.DMA((6,)),
            pltpu.SemaphoreType.DMA((th // SPAN,)),
            pltpu.SemaphoreType.DMA((8,)),
            pltpu.SemaphoreType.DMA((8,)),
        ],
        compiler_params=pltpu.CompilerParams(collective_id=0, has_side_effects=True, vmem_limit_bytes=36 * 2**20),
        cost_estimate=pl.CostEstimate(
            flops=2 * 6 * th * tw * c * c, bytes_accessed=2 * th * tw * c, transcendentals=th * tw * c
        ),
        name="interior",
    )(image, proj_in, taps_wide, taps_tall, proj_out, bias)


def border_kernel(centre, done, last_l, last_r, weights, bias, out, block, out_sem):
    th = done.shape[0]
    tw = done.shape[1]
    inner = pl.ds(2, th - SPAN)
    copies = [pltpu.make_async_copy(done.at[inner], out.at[inner], out_sem.at[0])]
    copies[0].start()
    half = 0.5 * bias[...]
    first = [0] + [th - SPAN + 2 * q for q in range(1, PAIRS)]

    def pick(side, q, i):
        if side == 1:
            return centre[first[q] + i]
        return (last_l, None, last_r)[side][(2 * q + 2 if q else 0) + i]

    for i, y in enumerate(products(pick, weights)):
        y = activated(y + half)
        for q in range(PAIRS):
            block[2 * q + i] = (centre[first[q] + i + 1].astype(F32) + y[q * tw : (q + 1) * tw]).astype(BF16)
    copies.append(pltpu.make_async_copy(block.at[pl.ds(0, 2)], out.at[pl.ds(0, 2)], out_sem.at[1]))
    copies.append(
        pltpu.make_async_copy(block.at[pl.ds(2, SPAN - 2)], out.at[pl.ds(th - SPAN + 2, SPAN - 2)], out_sem.at[2])
    )
    for copy in copies[1:]:
        copy.start()
    for copy in copies:
        copy.wait()


def border(centre, done, last_l, last_r, weights, bias):
    th, tw, c = done.shape
    vmem, hbm = pl.BlockSpec(memory_space=pltpu.VMEM), pl.BlockSpec(memory_space=pltpu.HBM)
    return pl.pallas_call(
        border_kernel,
        out_shape=jax.ShapeDtypeStruct((th, tw, c), BF16),
        in_specs=[vmem] * 6,
        out_specs=hbm,
        scratch_shapes=[pltpu.VMEM((SPAN, tw, c), BF16), pltpu.SemaphoreType.DMA((3,))],
        compiler_params=pltpu.CompilerParams(vmem_limit_bytes=24 * 2**20),
        cost_estimate=pl.CostEstimate(
            flops=2 * 6 * SPAN * tw * c * c, bytes_accessed=2 * th * tw * c, transcendentals=SPAN * tw * c
        ),
        name="border",
    )(centre, done, last_l, last_r, weights, bias)


def solution(mesh):
    rows, cols = mesh.shape["row"], mesh.shape["col"]

    def on_device(image, proj_in, taps_wide, taps_tall, proj_out, bias):
        bias = bias[None, :]
        held = [pltpu.with_memory_space_constraint(x, pltpu.HBM) for x in (image, proj_in, taps_wide, taps_tall, proj_out)]
        return border(*interior(rows, cols, *held, bias), bias)

    in_specs = (P("row", "col", None), P(), P(), P(), P(), P())
    out_specs = P("row", "col", None)
    return jax.shard_map(on_device, mesh=mesh, in_specs=in_specs, out_specs=out_specs, check_vma=False)
```

time: 85.5 us -> 24.9 us (0.29)
  the two profiles are of different devices: /device:TPU:77 before, /device:TPU:32 now
where the time goes in v2:
time: 24.9 us; the launch traced here: 24.8 us
  Pallas kernels  24.1 us (97%)
  local copies, waits for them, and re-layouts  0.68 us (3%)
    pallas_call x1, Pallas kernels, interior(): pl.pallas_call(functools.partial(interior_kernel, rows, cols), out_shape=...  21.4 us
    pallas_call x1, Pallas kernels, border(): pl.pallas_call(border_kernel, out_shape=jax.ShapeDtypeStruct((th, tw, c),...  2.72 us
    unnamed x2, local copies, waits for them, and re-layouts  0.68 us

profile of v2, /device:TPU:32, one launch (start us, length us, event | category | flops | bytes accessed | tf_op | source)
XLA Modules:
  0.0 24.8 jit_solution(5133701525485128976)
XLA Ops:
  0.0 0.0 copy-start
  0.0 0.7 %copy-done = f32[256]{0:T(256)S(1)} copy-done((f32[256]{0:T(256)S(1)}, f32[256]{0:T(256)}, u32[]{:S(2)}) %copy-start) | copy-done | bytes 1048
  0.7 21.4 %interior.1 = (bf16[50,256,256]{2,1,0:T(8,128)(2,1)S(1)}, bf16[48,256,256]{2,1,0:T(8,128)(2,1)S(1)}, bf16[10,256,256]{2,1,0:T(8,128)(2,1)S(1)}, bf16[10,256,256]...) custom-call(bf16[48,256,256]{2,1,0:T(8,128)(2,1)} %image.1, bf16[256,512]{1,0:T(8,128)(2,1)} %proj_in.1, f32[3,512]{1,0:T(4,128)} %taps_wide.1, ...), custom_call_target="tpu_custom_call" | custom-call | flops 9663676416 | bytes 6291456 | tf_op jit(solution)/shard_map/interior/pallas_call | solution.py:275
  22.1 2.7 %border.1 = bf16[48,256,256]{2,1,0:T(8,128)(2,1)} custom-call(bf16[50,256,256]{2,1,0:T(8,128)(2,1)S(1)} %get-tuple-element.10.centre, bf16[48,256,256]{2,1,0:T(8,128)(2,1)S(1)} %get-tuple-element.11.done, bf16[10,256,256]{2,1,0:T(8,128)(2,1)S(1)} %get-tuple-element.12.last_l, bf16[10,256,256]{2,1,0:T(8,128)(2,1)S(1)} %get-tuple-element.13.last_r, ...), custom_call_target="tpu_custom_call" | custom-call | flops 1207959552 | bytes 6291456 | tf_op jit(solution)/shard_map/border/pallas_call | solution.py:343
Async XLA Ops:
  0.0 0.7 %copy-start = (f32[256]{0:T(256)S(1)}, f32[256]{0:T(256)}, u32[]{:S(2)}) copy-start(f32[256]{0:T(256)} %param.11) | copy-start | bytes 3076

commit v3 on v0

v3 whole, which is shorter than its diff:
```python
import functools

import jax
import jax.numpy as jnp
from jax import lax
from jax.experimental import pallas as pl
from jax.experimental.pallas import tpu as pltpu
from jax.sharding import PartitionSpec as P

MESH = pl.DeviceIdType.MESH
F32, BF16 = jnp.float32, jnp.bfloat16
EDGE = 16
PAIRS = 3
SPAN = 2 * PAIRS
DEEP = SPAN + 2
PARTS = 4
BLOCK = 128
ROWS_OF = ((0, 2), (1, 2), (2, 1), (1, 3))


def interleave(*queues):
    pieces = [((i + 0.5) / len(queue), n, i) for n, queue in enumerate(queues) for i in range(len(queue))]
    for _, n, i in sorted(pieces):
        queues[n][i]()


def get_rows(ref, at):
    return jnp.concatenate([ref[n, at] for n in range(ref.shape[0])], 1)


def put_rows(ref, at, value):
    wide = ref.shape[2]
    for n in range(ref.shape[0]):
        ref[n, at] = value[:, n * wide : (n + 1) * wide]


def activated(t):
    return t + t * jnp.tanh(t)


def shifted(v, before, after):
    p = jnp.concatenate([v[1:], after], 0)
    return jnp.concatenate([before, v[:1], p[:-2]], 0), p


def product_pieces(pick, weights, half, total):
    c = weights.shape[2]
    state = {}

    def part(k, side):
        a, b = ROWS_OF[k]
        rows = [(pick(side, q, a), pick(side, q, b)) for q in range(PAIRS)]
        moved = jnp.concatenate([x + y if k == 1 else x - y for x, y in rows], 0)
        m = jnp.dot(moved, weights[k, side * c : (side + 1) * c], preferred_element_type=F32)
        state[k] = m if side == 0 else state[k] + m
        if side < 2:
            return
        if k == 2:
            m1 = state[1] + half[...]
            total[0] = m1 + state[2]
            total[1] = m1 - state[2]
        elif k == 0:
            total[0] = total[0] + state[0]
        elif k == 3:
            total[1] = total[1] - state[3]

    return [functools.partial(part, k, side) for two in ((1, 2), (0, 3)) for side in range(3) for k in two]


def interior_kernel(
    rows, cols,
    image, proj_in, taps_wide, taps_tall, proj_out, bias,
    done, top, bottom, halo_l, halo_r, corners, edge_l, edge_r, ends, before_l, before_r, kept, weights, half,
    centre, left_a, left_b, right_a, right_b, sum_a, sum_b, p_in, t_wide, t_tall, p_out, b_in,
    local_sem, stage_sem, send_sem, recv_sem,
):
    th, tw, c = image.shape
    steps = th // SPAN
    r, k = lax.axis_index("row"), lax.axis_index("col")
    up, down = lax.rem(r + rows - 1, rows), lax.rem(r + 1, rows)
    west, east = lax.rem(k + cols - 1, cols), lax.rem(k + 1, cols)
    above, below, before, behind = r > 0, r < rows - 1, k > 0, k < cols - 1
    around = [
        ((up, k), above), ((down, k), below), ((r, west), before), ((r, east), behind),
        ((up, west), above & before), ((down, east), below & behind), ((up, east), above & behind), ((down, west), below & before),
    ]

    barrier = pltpu.get_barrier_semaphore()
    for to, there in around:

        @pl.when(there)
        def _():
            pl.semaphore_signal(barrier, inc=1, device_id=to, device_id_type=MESH)

    def stage(s):
        return pltpu.make_async_copy(image.at[pl.ds(s * SPAN, SPAN)], centre.at[pl.ds(1 + s * SPAN, SPAN)], stage_sem.at[s])

    local = [
        pltpu.make_async_copy(src, dst, local_sem.at[i])
        for i, (src, dst) in enumerate(
            [(proj_in, p_in), (taps_wide, t_wide), (taps_tall, t_tall), (proj_out, p_out), (bias, b_in)]
        )
    ]
    for copy in local:
        copy.start()
    for s in range(steps):
        stage(s).start()

    zero = jnp.zeros((1, c), BF16)
    centre[0] = jnp.zeros((tw, c), BF16)
    centre[th + 1] = jnp.zeros((tw, c), BF16)

    def shift(at, left, right, i):
        left[i], right[i] = shifted(centre[at], zero, zero)

    for copy in local:
        copy.wait()
    half[...] = 0.5 * b_in[...]
    for s in range(2):
        stage(s).wait()

    base = p_in[...].astype(F32)
    g, split = {}, {}

    def scale(j, i):
        a = base * (0.25 * t_wide[pl.ds(j, 1)] * t_tall[pl.ds(i, 1)])
        high = a.astype(BF16)
        split[j, i] = high, (a - high.astype(F32)).astype(BF16)

    def weigh(j, i):
        high, low = split.pop((j, i))
        g[i] = jnp.dot(high, p_out[...], preferred_element_type=F32) + jnp.dot(low, p_out[...], preferred_element_type=F32)
        if i < 2:
            return
        at = pl.ds(j * c, c)
        ends = g[0] + g[2]
        weights[0, at] = (g[0] + g[0]).astype(BF16)
        weights[1, at] = (ends + g[1]).astype(BF16)
        weights[2, at] = (ends - g[1]).astype(BF16)
        weights[3, at] = (g[2] + g[2]).astype(BF16)

    taps = [(j, i) for j in range(3) for i in range(3)]
    scale(*taps[0])
    making = []
    for n, tap in enumerate(taps):
        if n + 1 < len(taps):
            making.append(functools.partial(scale, *taps[n + 1]))
        making.append(functools.partial(weigh, *tap))
    interleave(making, [functools.partial(shift, i, left_a, right_a, i) for i in range(DEEP)])

    def multiply(s, left, right, total):
        def pick(side, q, i):
            if side == 1:
                return centre[SPAN * s + 2 * q + i]
            return (left, None, right)[side][2 * q + i]

        return product_pieces(pick, weights, half, total)

    def finish(s, total, slots):
        def part(q, i, n):
            row = SPAN * s + 2 * q + i
            pair = pl.ds(PAIRS * s + q, 1)
            across = pl.ds(n * BLOCK, BLOCK)
            t = total[i, pl.ds(q * tw + n * BLOCK, BLOCK)]
            done[row, across] = (centre[row + 1, across].astype(F32) + activated(t)).astype(BF16)
            if n == 0:
                before_l[i, pair] = t[:1]
            if n == tw // BLOCK - 1:
                before_r[i, pair] = t[BLOCK - 1 :]
            if (q, i) == (0, 0) and slots[0] is not None:
                kept[slots[0], across] = t
            if (q, i) == (PAIRS - 1, 1) and slots[1] is not None:
                kept[slots[1], across] = t

        return [functools.partial(part, q, i, n) for i in range(2) for q in range(PAIRS) for n in range(tw // BLOCK)]

    def prepare(s, left, right, old_left, old_right):
        def again(i):
            left[i] = old_left[SPAN + i]
            right[i] = old_right[SPAN + i]

        return [functools.partial(again, i) for i in range(2)] + [
            functools.partial(shift, SPAN * s + i, left, right, i) for i in range(2, DEEP)
        ]

    stage(2).wait()
    interleave(multiply(0, left_a, right_a, sum_a), prepare(1, left_b, right_b, left_a, right_a))
    for s in range(3, steps):
        stage(s).wait()

    ends[0] = centre[1]
    ends[1] = centre[th]
    edge_l[...] = centre[pl.ds(1, th), pl.ds(0, EDGE)][:, 0]
    edge_r[...] = centre[pl.ds(1, th), pl.ds(tw - EDGE, EDGE)][:, EDGE - 1]
    pl.semaphore_wait(barrier, sum(there.astype(jnp.int32) for _, there in around))

    first, last = pl.ds(0, EDGE), pl.ds(th - EDGE, EDGE)
    moves = [
        (centre.at[1], bottom),
        (centre.at[th], top),
        (edge_l, halo_r),
        (edge_r, halo_l),
        (edge_l.at[first], corners.at[0]),
        (edge_r.at[last], corners.at[3]),
        (edge_r.at[first], corners.at[1]),
        (edge_l.at[last], corners.at[2]),
    ]
    copies = [
        pltpu.make_async_remote_copy(
            src_ref=src, dst_ref=dst, send_sem=send_sem.at[i], recv_sem=recv_sem.at[i], device_id=around[i][0], device_id_type=MESH
        )
        for i, (src, dst) in enumerate(moves)
    ]
    for copy, (_, there) in zip(copies, around):
        pl.when(there)(copy.start)

    def two(n, carry):
        s = 2 * n + 1
        interleave(
            multiply(s, left_b, right_b, sum_b),
            finish(s - 1, sum_a, (jnp.minimum(n, 1), None)),
            prepare(s + 1, left_a, right_a, left_b, right_b),
        )
        interleave(
            multiply(s + 1, left_a, right_a, sum_a),
            finish(s, sum_b, (None, None)),
            prepare(s + 2, left_b, right_b, left_a, right_a),
        )
        return carry

    lax.fori_loop(0, (steps - 2) // 2, two, 0)
    interleave(multiply(steps - 1, left_b, right_b, sum_b), finish(steps - 2, sum_a, (None, None)))
    interleave(finish(steps - 1, sum_b, (None, 2)))

    def clear(ref):
        ref[...] = jnp.zeros(ref.shape, ref.dtype)

    for i, (copy, (_, there)) in enumerate(zip(copies, around)):
        pl.when(there)(copy.wait_send)
        comes = around[i ^ 1][1]
        pl.when(comes)(copy.wait_recv)
        pl.when(jnp.logical_not(comes))(functools.partial(clear, moves[i][1]))


def interior(rows, cols, image, proj_in, taps_wide, taps_tall, proj_out, bias):
    th, tw, c = image.shape
    rank = proj_in.shape[1]
    pairs = -(-th // 32) * 16
    vmem, hbm = pl.BlockSpec(memory_space=pltpu.VMEM), pl.BlockSpec(memory_space=pltpu.HBM)
    shape = jax.ShapeDtypeStruct
    out_shape = (
        shape((th, tw, c), BF16),
        *[shape((tw, c), BF16)] * 2,
        *[shape((th, c), BF16)] * 2,
        shape((4, EDGE, c), BF16),
        *[shape((th, c), BF16)] * 2,
        shape((2, tw, c), BF16),
        *[shape((2, pairs, c), F32)] * 2,
        shape((3, tw, c), F32),
        shape((4, 3 * c, c), BF16),
        shape((1, c), F32),
    )
    return pl.pallas_call(
        functools.partial(interior_kernel, rows, cols),
        out_shape=out_shape,
        in_specs=[hbm] * 6,
        out_specs=(vmem,) * len(out_shape),
        scratch_shapes=[pltpu.VMEM((th + 2, tw, c), BF16)]
        + [pltpu.VMEM((DEEP, tw, c), BF16)] * 4
        + [pltpu.VMEM((2, PAIRS * tw, c), F32)] * 2
        + [
            pltpu.VMEM((c, rank), BF16),
            pltpu.VMEM((3, rank), F32),
            pltpu.VMEM((3, rank), F32),
            pltpu.VMEM((rank, c), BF16),
            pltpu.VMEM((1, c), F32),
            pltpu.SemaphoreType.DMA((5,)),
            pltpu.SemaphoreType.DMA((th // SPAN,)),
            pltpu.SemaphoreType.DMA((8,)),
            pltpu.SemaphoreType.DMA((8,)),
        ],
        compiler_params=pltpu.CompilerParams(collective_id=0, has_side_effects=True, vmem_limit_bytes=44 * 2**20),
        cost_estimate=pl.CostEstimate(
            flops=2 * 6 * th * tw * c * c, bytes_accessed=2 * th * tw * c, transcendentals=th * tw * c
        ),
        name="interior",
    )(image, proj_in, taps_wide, taps_tall, proj_out, bias)


def border_kernel(
    done, top, bottom, halo_l, halo_r, corners, edge_l, edge_r, ends, before_l, before_r, kept, weights, half,
    out,
    block, strip_l, strip_r, column, own, new_l, new_r, add_l, add_r, out_sem,
):
    th, tw, c = done.shape
    pairs = before_l.shape[1]
    inner_rows, inner_cols = pl.ds(1, th - 2), pl.ds(EDGE, tw - 2 * EDGE)
    low, high = pl.ds(0, EDGE), pl.ds(tw - EDGE, EDGE)
    bounds = [1 + (th - 2) * i // PARTS for i in range(PARTS + 1)]
    copies = []
    for i in range(PARTS):
        at = pl.ds(bounds[i], bounds[i + 1] - bounds[i])
        copies.append(pltpu.make_async_copy(done.at[at, inner_cols], out.at[at, inner_cols], out_sem.at[4 + i]))
    for copy in copies:
        copy.start()

    column[...] = jnp.zeros_like(column)
    own[...] = jnp.zeros_like(own)
    for halo, edge, before, new, add, at in (
        (halo_l, edge_l, before_l, new_l, add_l, 0),
        (halo_r, edge_r, before_r, new_r, add_r, 2 * c),
    ):
        put_rows(column, pl.ds(8, th), halo[...].astype(F32))
        put_rows(own, pl.ds(0, th), edge[...].astype(F32))
        d = [get_rows(column, pl.ds(7 + i, pairs, stride=2)) for i in range(4)]
        m = [
            jnp.dot(v.astype(BF16), weights[i, pl.ds(at, c)], preferred_element_type=F32)
            for i, v in enumerate([d[0] - d[2], d[1] + d[2], d[2] - d[1], d[1] - d[3]])
        ]
        for i, y in enumerate([m[0] + m[1] + m[2], m[1] - m[2] - m[3]]):
            lines = pl.ds(i, pairs, stride=2)
            put_rows(add, lines, y)
            put_rows(new, lines, get_rows(own, lines) + activated(before[i] + y))

    line = lax.broadcasted_iota(jnp.int32, (EDGE, c), 0)
    is_first, is_last = (line == 0).astype(F32).astype(BF16), (line == EDGE - 1).astype(F32).astype(BF16)
    not_first, not_last = 1 - is_first, 1 - is_last
    for h in range(1, th - 1):
        strip_l[h] = done[h, low] * not_first + get_rows(new_l, pl.ds(h, 1)).astype(BF16) * is_first
        strip_r[h] = done[h, high] * not_last + get_rows(new_r, pl.ds(h, 1)).astype(BF16) * is_last
    copies += [
        pltpu.make_async_copy(strip_l.at[inner_rows], out.at[inner_rows, low], out_sem.at[0]),
        pltpu.make_async_copy(strip_r.at[inner_rows], out.at[inner_rows, high], out_sem.at[1]),
    ]
    for copy in copies[PARTS:]:
        copy.start()

    across = lax.broadcasted_iota(jnp.int32, (tw, c), 0)
    own_rows = (0, th - 1)
    for i, (halo, weight, from_l, from_r, at, slot) in enumerate([
        (top, 0, 3, 2, EDGE - 1, 0),
        (bottom, 3, 1, 0, 0, 2),
    ]):
        row = own_rows[i]
        v = halo[...]
        left, right = shifted(v, corners[from_l][at : at + 1], corners[from_r][at : at + 1])
        t = kept[slot] + jnp.dot(jnp.concatenate([left, v, right], 1), weights[weight], preferred_element_type=F32)
        t = t + jnp.where(across == 0, get_rows(add_l, pl.ds(row, 1)), 0.0)
        t = t + jnp.where(across == tw - 1, get_rows(add_r, pl.ds(row, 1)), 0.0)
        block[i] = (ends[i].astype(F32) + activated(t)).astype(BF16)
        copy = pltpu.make_async_copy(block.at[i], out.at[row], out_sem.at[2 + i])
        copy.start()
        copies.append(copy)
    for copy in copies:
        copy.wait()


def border(done, *others):
    th, tw, c = done.shape
    pairs = -(-th // 32) * 16
    halves = c // 128
    vmem, hbm = pl.BlockSpec(memory_space=pltpu.VMEM), pl.BlockSpec(memory_space=pltpu.HBM)
    return pl.pallas_call(
        border_kernel,
        out_shape=jax.ShapeDtypeStruct((th, tw, c), BF16),
        in_specs=[vmem] * (1 + len(others)),
        out_specs=hbm,
        scratch_shapes=[pltpu.VMEM((2, tw, c), BF16)]
        + [pltpu.VMEM((th, EDGE, c), BF16)] * 2
        + [pltpu.VMEM((halves, 2 * pairs + 16, 128), F32)]
        + [pltpu.VMEM((halves, 2 * pairs, 128), F32)] * 5
        + [pltpu.SemaphoreType.DMA((4 + PARTS,))],
        compiler_params=pltpu.CompilerParams(vmem_limit_bytes=16 * 2**20),
        cost_estimate=pl.CostEstimate(
            flops=2 * 2 * 3 * tw * c * c, bytes_accessed=2 * th * tw * c, transcendentals=2 * tw * c
        ),
        name="border",
    )(done, *others)


def solution(mesh):
    rows, cols = mesh.shape["row"], mesh.shape["col"]

    def on_device(image, proj_in, taps_wide, taps_tall, proj_out, bias):
        given = (image, proj_in, taps_wide, taps_tall, proj_out, bias[None, :])
        return border(*interior(rows, cols, *[pltpu.with_memory_space_constraint(x, pltpu.HBM) for x in given]))

    in_specs = (P("row", "col", None), P(), P(), P(), P(), P())
    out_specs = P("row", "col", None)
    return jax.shard_map(on_device, mesh=mesh, in_specs=in_specs, out_specs=out_specs, check_vma=False)
```

time: 85.5 us -> 22.3 us (0.26)
  the two profiles are of different devices: /device:TPU:77 before, /device:TPU:46 now
where the time goes in v3:
time: 22.3 us; the launch traced here: 22.2 us
  Pallas kernels  22.2 us (100%)
    pallas_call x1, Pallas kernels, interior(): pl.pallas_call(functools.partial(interior_kernel, rows, cols), out_shape=...  19 us
    pallas_call x1, Pallas kernels, border(): pl.pallas_call(border_kernel, out_shape=jax.ShapeDtypeStruct((th, tw, c),...  3.27 us

profile of v3, /device:TPU:46, one launch (start us, length us, event | category | flops | bytes accessed | tf_op | source)
XLA Modules:
  0.0 22.2 jit_solution(15478758687285964126)
XLA Ops:
  0.0 19.0 %interior.1 = (bf16[48,256,256]{2,1,0:T(8,128)(2,1)S(1)}, bf16[256,256]{1,0:T(8,128)(2,1)S(1)}, bf16[256,256]{1,0:T(8,128)(2,1)S(1)}, bf16[48,256]{1,0:T(8,128)(...) custom-call(bf16[48,256,256]{2,1,0:T(8,128)(2,1)} %image.1, ...), custom_call_target="tpu_custom_call" | custom-call | flops 9663676416 | bytes 6291456 | tf_op jit(solution)/shard_map/interior/pallas_call | solution.py:263
  19.0 3.3 %border.1 = bf16[48,256,256]{2,1,0:T(8,128)(2,1)} custom-call(bf16[48,256,256]{2,1,0:T(8,128)(2,1)S(1)} %get-tuple-element.19.done, bf16[256,256]{1,0:T(8,128)(2,1)S(1)} %get-tuple-element.20.top, bf16[256,256]{1,0:T(8,128)(2,1)S(1)} %get-tuple-element.21.bottom, bf16[48,256]{1,0:T(8,128)(2,1)S(1)} %get-tuple-element.22.halo_l, ...), custom_call_target="tpu_custom_call" | custom-call | flops 201326592 | bytes 6291456 | tf_op jit(solution)/shard_map/border/pallas_call | solution.py:363

commit v4 on v3

--- a/solution.py
+++ b/solution.py
@@ -85,13 +85,6 @@
         ((up, west), above & before), ((down, east), below & behind), ((up, east), above & behind), ((down, west), below & before),
     ]
 
-    barrier = pltpu.get_barrier_semaphore()
-    for to, there in around:
-
-        @pl.when(there)
-        def _():
-            pl.semaphore_signal(barrier, inc=1, device_id=to, device_id_type=MESH)
-
     def stage(s):
         return pltpu.make_async_copy(image.at[pl.ds(s * SPAN, SPAN)], centre.at[pl.ds(1 + s * SPAN, SPAN)], stage_sem.at[s])
 
@@ -105,6 +98,13 @@
         copy.start()
     for s in range(steps):
         stage(s).start()
+
+    barrier = pltpu.get_barrier_semaphore()
+    for to, there in around:
+
+        @pl.when(there)
+        def _():
+            pl.semaphore_signal(barrier, inc=1, device_id=to, device_id_type=MESH)
 
     zero = jnp.zeros((1, c), BF16)
     centre[0] = jnp.zeros((tw, c), BF16)
@@ -211,8 +211,8 @@
         )
         for i, (src, dst) in enumerate(moves)
     ]
-    for copy, (_, there) in zip(copies, around):
-        pl.when(there)(copy.start)
+    for i in (4, 5, 6, 7, 2, 3, 0, 1):
+        pl.when(around[i][1])(copies[i].start)
 
     def two(n, carry):
         s = 2 * n + 1

time: 22.3 us -> 21.7 us (0.973); the launches traced: 22.2 us -> 21.4 us
  Pallas kernels: 22.2 us -> 21.4 us
    pallas_call x1, Pallas kernels: 19 us -> 18.1 us  [interior(): pl.pallas_call(functools.partial(interior_kernel, rows, cols), out_shape=...]
where the time goes in v4:
time: 21.7 us; the launch traced here: 21.4 us
  Pallas kernels  21.4 us (99%)
    pallas_call x1, Pallas kernels, interior(): pl.pallas_call(functools.partial(interior_kernel, rows, cols), out_shape=...  18.1 us
    pallas_call x1, Pallas kernels, border(): pl.pallas_call(border_kernel, out_shape=jax.ShapeDtypeStruct((th, tw, c),...  3.27 us

profile of v4, /device:TPU:46, one launch (start us, length us, event | category | flops | bytes accessed | tf_op | source)
XLA Modules:
  0.0 21.4 jit_solution(724660508296330918)
XLA Ops:
  0.0 18.1 %interior.1 = (bf16[48,256,256]{2,1,0:T(8,128)(2,1)S(1)}, bf16[256,256]{1,0:T(8,128)(2,1)S(1)}, bf16[256,256]{1,0:T(8,128)(2,1)S(1)}, bf16[48,256]{1,0:T(8,128)(...) custom-call(bf16[48,256,256]{2,1,0:T(8,128)(2,1)} %image.1, ...), custom_call_target="tpu_custom_call" | custom-call | flops 9663676416 | bytes 6291456 | tf_op jit(solution)/shard_map/interior/pallas_call | solution.py:263
  18.1 3.3 %border.1 = bf16[48,256,256]{2,1,0:T(8,128)(2,1)} custom-call(bf16[48,256,256]{2,1,0:T(8,128)(2,1)S(1)} %get-tuple-element.19.done, bf16[256,256]{1,0:T(8,128)(2,1)S(1)} %get-tuple-element.20.top, bf16[256,256]{1,0:T(8,128)(2,1)S(1)} %get-tuple-element.21.bottom, bf16[48,256]{1,0:T(8,128)(2,1)S(1)} %get-tuple-element.22.halo_l, ...), custom_call_target="tpu_custom_call" | custom-call | flops 201326592 | bytes 6291456 | tf_op jit(solution)/shard_map/border/pallas_call | solution.py:363

commit v5 on v4

--- a/solution.py
+++ b/solution.py
@@ -116,8 +116,6 @@
     for copy in local:
         copy.wait()
     half[...] = 0.5 * b_in[...]
-    for s in range(2):
-        stage(s).wait()
 
     base = p_in[...].astype(F32)
     g, split = {}, {}
@@ -146,7 +144,11 @@
         if n + 1 < len(taps):
             making.append(functools.partial(scale, *taps[n + 1]))
         making.append(functools.partial(weigh, *tap))
-    interleave(making, [functools.partial(shift, i, left_a, right_a, i) for i in range(DEEP)])
+    ahead = len(making) // 3
+    interleave(making[:ahead])
+    for s in range(2):
+        stage(s).wait()
+    interleave(making[ahead:], [functools.partial(shift, i, left_a, right_a, i) for i in range(DEEP)])
 
     def multiply(s, left, right, total):
         def pick(side, q, i):

time: 21.7 us -> 21.8 us (level)
  no operation moved by 1% of the time
where the time goes in v5:
time: 21.8 us; the launch traced here: 21.4 us
  Pallas kernels  21.4 us (98%)
    pallas_call x1, Pallas kernels, interior(): pl.pallas_call(functools.partial(interior_kernel, rows, cols), out_shape=...  18.1 us
    pallas_call x1, Pallas kernels, border(): pl.pallas_call(border_kernel, out_shape=jax.ShapeDtypeStruct((th, tw, c),...  3.27 us

profile of v5, /device:TPU:46, one launch (start us, length us, event | category | flops | bytes accessed | tf_op | source)
XLA Modules:
  0.0 21.4 jit_solution(8094384266075098411)
XLA Ops:
  0.0 18.1 %interior.1 = (bf16[48,256,256]{2,1,0:T(8,128)(2,1)S(1)}, bf16[256,256]{1,0:T(8,128)(2,1)S(1)}, bf16[256,256]{1,0:T(8,128)(2,1)S(1)}, bf16[48,256]{1,0:T(8,128)(...) custom-call(bf16[48,256,256]{2,1,0:T(8,128)(2,1)} %image.1, ...), custom_call_target="tpu_custom_call" | custom-call | flops 9663676416 | bytes 6291456 | tf_op jit(solution)/shard_map/interior/pallas_call | solution.py:265
  18.1 3.3 %border.1 = bf16[48,256,256]{2,1,0:T(8,128)(2,1)} custom-call(bf16[48,256,256]{2,1,0:T(8,128)(2,1)S(1)} %get-tuple-element.19.done, bf16[256,256]{1,0:T(8,128)(2,1)S(1)} %get-tuple-element.20.top, bf16[256,256]{1,0:T(8,128)(2,1)S(1)} %get-tuple-element.21.bottom, bf16[48,256]{1,0:T(8,128)(2,1)S(1)} %get-tuple-element.22.halo_l, ...), custom_call_target="tpu_custom_call" | custom-call | flops 201326592 | bytes 6291456 | tf_op jit(solution)/shard_map/border/pallas_call | solution.py:365
